TPU v7x, 256 devices: a whole 4x4x8 slice. The times are simulated.
256 devices in a mesh: blk: 16 (over x, y_lo, core), rep: 16 (over y_hi, z).
Axes of the slice: x: 4, y: 4 (y_hi: 2, y_lo: 2; y = y_hi * 2 + y_lo), z: 8, core: 2. Of those that a mesh axis runs over, the one named last changes fastest.
Arguments:
- kinematics: float32 [6, 65536], P(None, 'blk'), may hold values from -6 to 6
- derivatives: float32 [6, 65536], P(None, 'blk'), may hold values from -6 to 6
- masses: float32 [65536], P('blk'), may hold values from 0.2 to 5
- last_time: float32 [65536], P('blk'), may hold values from -0.25 to -0.0625
- block_list: int32 [2, 16, 16, 2], replicated, may hold values from 0 to 31, as said below
- block_count: int32 [2, 16, 16], replicated, may hold values from 0 to 2, as said below
Outputs:
- new_kinematics: float32 [6, 65536], P(None, 'blk')
- new_derivatives: float32 [6, 65536], P(None, 'blk')
Inputs may be any that keep to these rules, and one draw needn't show every extreme that they name: `block_list`: for each step and blk index the 32 listed block numbers are distinct. Slots at or past a device's count are ignored. `block_count`: in every step some device's count is 2.
All inputs are finite; a program needn't handle non-finite values.
Results may differ from a plain program's by a relative error of at most 0.0003.
Values sent between devices are 32-bit elements; how exact they have to be, the bound alone decides.
No kernel may reach another device: no remote copies, remote signals or barrier semaphores. Data moves between devices by JAX's collectives and lax.ppermute only.
A program may use at most 64 MiB of HBM per device.

v0:
```python
import functools

import jax
import jax.numpy as jnp
from jax import lax
from jax.experimental import pallas as pl
from jax.experimental.pallas import tpu as pltpu
from jax.sharding import PartitionSpec as P

BLOCK = 128
CAP = 2
STEPS = 2
ROWS = 8
F32 = jnp.float32
BF16 = jnp.bfloat16

step_length = 0.125
softening = 0.0025
grid_shift = 1.5 * 2.0**16
piece_rows = 128
chunk = 256
ahead_chunk = 1024
early_chunks = 2
early_pair = 2
prep_width = 512
first_slots = 12


def predict(position, velocity, acceleration, jerk_old, interval):
    new_position = position + interval * (
        velocity + interval * (acceleration * 0.5 + interval * jerk_old / 6.0)
    )
    new_velocity = velocity + interval * (acceleration + interval * jerk_old * 0.5)
    return jnp.concatenate([new_position, new_velocity], axis=0)


def correct(predicted, old_deriv, forces, interval):
    change = old_deriv[:3] - forces[:3]
    second_term = -6.0 * change - interval * (4.0 * old_deriv[3:] + 2.0 * forces[3:])
    third_term = 12.0 * change + 6.0 * interval * (old_deriv[3:] + forces[3:])
    new_position = predicted[:3] + interval * interval * (second_term / 24.0 + third_term / 120.0)
    new_velocity = predicted[3:] + interval * (second_term / 6.0 + third_term / 24.0)
    return jnp.concatenate([new_position, new_velocity], axis=0)


def round_short(value):
    return value.astype(BF16).astype(F32)


def split_three(value):
    high = round_short(value)
    rest = value - high
    middle = round_short(rest)
    return high, middle, rest - middle


def stack_three(value):
    return jnp.concatenate(split_three(value), axis=0)


def star_pieces(stars):
    position, velocity = stars[0:3], stars[3:6]
    coarse = (position + grid_shift) - grid_shift
    coarse_a = round_short(coarse)
    coarse_b = coarse - coarse_a
    fine = position - coarse
    fine_a = round_short(fine)
    fine_b = round_short(fine - fine_a)
    fine = fine_a + fine_b
    square = jnp.sum(coarse * coarse, axis=0, keepdims=True)
    cross = jnp.sum(2.0 * coarse * fine + fine * fine, axis=0, keepdims=True)
    mixed = jnp.sum(position * velocity, axis=0, keepdims=True)
    return coarse_a, coarse_b, fine_a, fine_b, square, cross, mixed


def source_pieces(stars):
    ca, cb, fa, fb, square, cross, mixed = star_pieces(stars)
    va, vb, vc = split_three(stars[3:6])
    width = stars.shape[1]
    one = jnp.ones((3, width), F32)
    rows = [ca, ca, cb, cb, stack_three(square), one, jnp.zeros((6, width), F32)]
    rows += [ca, ca, cb, cb, fa, fa, fb, fb, fa, fa, stack_three(cross), one]
    rows += [va, va, va, vb, vb, vc, stack_three(mixed), one]
    rows += [jnp.zeros((piece_rows - 84, width), F32)]
    return jnp.concatenate(rows, axis=0)


def target_pieces(stars):
    ca, cb, fa, fb, square, cross, mixed = star_pieces(stars)
    va, vb, vc = split_three(stars[3:6])
    xa, xb, xc = split_three(stars[0:3])
    width = stars.shape[1]
    one = jnp.ones((3, width), F32)
    zero = jnp.zeros((3, width), F32)
    da, db = -2.0 * ca, -2.0 * cb
    ea, eb = -2.0 * fa, -2.0 * fb
    tail = jnp.zeros((piece_rows - 84, width), F32)
    radius = [da, db, da, db, one, stack_three(square), zero, zero]
    radius += [ea, eb, ea, eb, da, db, da, db, ea, eb, one, stack_three(cross + softening)]
    radius += [zero] * 8 + [tail]
    moving = [-va, -vb, -va, -vb, zero, zero, zero, zero]
    moving += [-vc, zero, zero, zero, -va, -vb, -va, zero, zero, zero, zero, zero]
    moving += [-xa, -xb, -xc, -xa, -xb, -xa, one, stack_three(mixed), tail]
    both = [jnp.concatenate(radius, axis=0), jnp.concatenate(moving, axis=0)]
    return jnp.concatenate(both, axis=1).astype(BF16)


def block_at(number):
    return pl.ds(pl.multiple_of(number * BLOCK, BLOCK), BLOCK)


def predicted_block(kin_ref, der_ref, last_ref, where, time_now):
    kin, der = kin_ref[:, where], der_ref[:, where]
    return predict(kin[:3], kin[3:], der[:3], der[3:], time_now - last_ref[:, where])


def list_place(step, blk, rep, slot, n_blk, n_rep):
    return ((step * n_blk + blk) * n_rep + rep) * CAP + slot


def write_targets(step, n_blk, n_rep, list_ref, kin_ref, der_ref, last_ref, out_ref):
    blk, rep = lax.axis_index("blk"), lax.axis_index("rep")
    rows = []
    for slot in range(CAP):
        number = list_ref[list_place(step, blk, rep, slot, n_blk, n_rep)]
        rows.append(predicted_block(kin_ref, der_ref, last_ref, block_at(number), step * step_length))
        rows.append(jnp.zeros((ROWS - 6, BLOCK), F32))
    mine = jnp.concatenate(rows, axis=0)
    for other in range(n_blk):
        out_ref[other] = mine


def targets_kernel(step, n_blk, n_rep, list_ref, kin_ref, der_ref, last_ref, out_ref):
    write_targets(step, n_blk, n_rep, list_ref, kin_ref, der_ref, last_ref, out_ref)


def forces_kernel(
    step, n_blk, n_rep, count_ref, target_ref, kin_ref, der_ref, last_ref, mass_ref,
    out_ref, pred_ref, piece_ref, moment_ref,
):
    rep = lax.axis_index("rep")
    width = kin_ref.shape[1]
    total = jnp.zeros((6, prep_width), F32)
    for part in range(width // prep_width):
        where = pl.ds(part * prep_width, prep_width)
        stars = predicted_block(kin_ref, der_ref, last_ref, where, step * step_length)
        pred_ref[:, where] = stars
        total = total + stars
    centre = jnp.sum(total, axis=1, keepdims=True) / width
    for part in range(width // prep_width):
        where = pl.ds(part * prep_width, prep_width)
        stars = pred_ref[:, where] - centre
        piece_ref[where, :] = source_pieces(stars).T.astype(BF16)
        scaled = mass_ref[:, where] / (width * n_blk)
        ones = jnp.ones((1, prep_width), F32)
        moments = jnp.concatenate([stars, ones, jnp.zeros_like(ones)], axis=0) * scaled
        moments = jnp.concatenate([stack_three(moments), jnp.zeros((8, prep_width), F32)], axis=0)
        moment_ref[:, where] = moments.astype(BF16)

    def one_slot(place, carry):
        blk = place // CAP
        slot = place % CAP
        active = slot < count_ref[(step * n_blk + blk) * n_rep + rep]

        @pl.when(active)
        def _():
            stars = target_ref[place][0:6] - centre
            against = target_pieces(stars)
            acc = jnp.zeros((32, 2 * BLOCK), F32)
            for part in range(width // chunk):
                where = pl.ds(part * chunk, chunk)
                both = jnp.dot(piece_ref[where, :], against, preferred_element_type=F32)
                inverse = lax.rsqrt(both[:, :BLOCK])
                inverse_sq = inverse * inverse
                weight = inverse * inverse_sq
                radial = weight * (inverse_sq * both[:, BLOCK:])
                pair = jnp.concatenate([weight, radial], axis=1)
                high = pair.astype(BF16)
                low = (pair - high.astype(F32)).astype(BF16)
                moments = moment_ref[:, where]
                acc = acc + jnp.dot(moments, high, preferred_element_type=F32)
                acc = acc + jnp.dot(moments, low, preferred_element_type=F32)
            acc = acc[0:8] + acc[8:16] + acc[16:24]
            by_weight, by_radial = acc[:, :BLOCK], acc[:, BLOCK:]
            sums = by_weight[0:6] - stars * by_weight[6:7]
            pull = by_radial[0:3] - stars[0:3] * by_radial[6:7]
            out_ref[place] = jnp.concatenate(
                [sums[0:3], sums[3:6] - 3.0 * pull, jnp.zeros((ROWS - 6, BLOCK), F32)], axis=0
            )

        @pl.when(jnp.logical_not(active))
        def _():
            out_ref[place] = jnp.zeros((ROWS, BLOCK), F32)

        return carry

    lax.fori_loop(0, n_blk * CAP, one_slot, 0)


def total_kernel(n_blk, n_rep, part_ref, out_ref):
    total = part_ref[0]
    for other in range(1, n_blk):
        total = total + part_ref[other]
    for other in range(n_rep):
        out_ref[other] = total


def update_kernel(
    step, n_blk, n_rep, list_ref, count_ref, force_ref, kin_ref, der_ref, last_ref,
    new_kin_ref, new_der_ref, new_last_ref, *next_refs,
):
    blk = lax.axis_index("blk")
    time_now = step * step_length
    new_kin_ref[...] = kin_ref[...]
    new_der_ref[...] = der_ref[...]
    new_last_ref[...] = last_ref[...]

    def one_slot(place, carry):
        rep = place // CAP
        slot = place % CAP

        @pl.when(slot < count_ref[(step * n_blk + blk) * n_rep + rep])
        def _():
            number = list_ref[list_place(step, blk, rep, slot, n_blk, n_rep)]
            where = block_at(number)
            predicted = predicted_block(kin_ref, der_ref, last_ref, where, time_now)
            forces = force_ref[place][0:6]
            interval = time_now - last_ref[:, where]
            new_kin_ref[:, where] = correct(predicted, der_ref[:, where], forces, interval)
            new_der_ref[:, where] = forces
            new_last_ref[:, where] = jnp.full((1, BLOCK), time_now, F32)

        return carry

    lax.fori_loop(0, n_rep * CAP, one_slot, 0)
    if next_refs:
        write_targets(
            step + 1, n_blk, n_rep, list_ref, new_kin_ref, new_der_ref, new_last_ref, next_refs[0]
        )


def lane_iota(rows):
    return lax.broadcasted_iota(jnp.int32, (rows, BLOCK), 1)


def active_rows(n_blk, n_rep, list_ref, count_ref):
    per_row = BLOCK // n_rep
    parts = BLOCK * n_rep // BLOCK // 4
    lanes = lane_iota(n_blk)
    steps = []
    for step in range(STEPS):
        counted = count_ref[step]
        tiled = []
        for slot in range(CAP):
            listed = jnp.where(counted > slot, list_ref[step, :, slot, :], -1)
            tiled.append(jnp.concatenate([listed] * per_row, axis=1))
        hits = []
        for part in range(parts):
            number = lanes // n_rep + part * per_row
            hit = (tiled[0] == number) | (tiled[1] == number)
            hits.append(jnp.where(hit, 1.0, 0.0))
        steps.append(jnp.concatenate(hits, axis=1))
    hits = jnp.concatenate(steps, axis=0).astype(BF16)
    width = parts * BLOCK
    rows = lax.broadcasted_iota(jnp.int32, (width, BLOCK), 0) // n_rep
    spread = jnp.where(rows == lax.broadcasted_iota(jnp.int32, (width, BLOCK), 1), 1.0, 0.0)
    return jnp.dot(hits, spread.astype(BF16), preferred_element_type=F32)


def share_blocks(n_blk, n_rep, list_ref, count_ref, table_ref):
    blk, rep = lax.axis_index("blk"), lax.axis_index("rep")
    flags = active_rows(n_blk, n_rep, list_ref, count_ref)
    first, second = flags[:n_blk], flags[n_blk:]
    in_both = first * second
    kinds = [in_both, first - in_both, second - in_both]
    earlier = lax.broadcasted_iota(jnp.int32, (BLOCK, BLOCK), 0) < lax.broadcasted_iota(
        jnp.int32, (BLOCK, BLOCK), 1
    )
    earlier = jnp.where(earlier, 1.0, 0.0).astype(BF16)
    above = lax.broadcasted_iota(jnp.int32, (n_blk, n_blk), 0) > lax.broadcasted_iota(
        jnp.int32, (n_blk, n_blk), 1
    )
    above = jnp.where(above, 1.0, 0.0).astype(BF16)
    own_row = lax.broadcasted_iota(jnp.int32, (n_blk, BLOCK), 0) == blk
    lanes = lane_iota(1)
    order = lanes * n_rep + rep
    start = jnp.zeros((1, 1), F32)
    fits = jnp.ones((1, 1), jnp.bool_)
    own_kind, own_place, own_rank, finish, owner = [], [], [], [], []
    for kind in kinds:
        short = kind.astype(BF16)
        rank = jnp.dot(short, earlier, preferred_element_type=F32)
        before = jnp.dot(above, short, preferred_element_type=F32)
        before = jnp.sum(before, axis=1, keepdims=True) + start
        amount = jnp.sum(kind, axis=1, keepdims=True)
        fits = fits & (jnp.max(amount, axis=0, keepdims=True) <= n_rep)
        ends = (before + amount).astype(jnp.int32)
        owner.append(jnp.sum(jnp.where(ends <= order, 1, 0), axis=0, keepdims=True))
        place = jnp.sum(jnp.where(own_row, before + rank, 0.0), axis=0, keepdims=True)
        own_place.append(place.astype(jnp.int32))
        own_rank.append(jnp.sum(jnp.where(own_row, rank, 0.0), axis=0, keepdims=True))
        own_kind.append(jnp.sum(jnp.where(own_row, kind, 0.0), axis=0, keepdims=True) > 0.5)
        finish.append((jnp.max(before + amount, axis=0, keepdims=True)).astype(jnp.int32))
        if len(finish) == 1:
            start = jnp.sum(amount, axis=0, keepdims=True)
    both_end = finish[0]
    total = [jnp.maximum(finish[0], finish[1]), jnp.maximum(finish[0], finish[2])]
    fits = fits & (total[0] <= n_rep * first_slots) & (total[1] <= n_rep * n_rep)
    handler = [jnp.bitwise_and(place, n_rep - 1) for place in own_place]
    home = []
    for step in range(STEPS):
        code = jnp.where(own_kind[0], handler[0] * 2, -1)
        home.append(jnp.where(own_kind[1 + step], handler[1 + step] * 2 + 1, code))
    places = []
    for step in range(STEPS):
        is_both = order < both_end
        places.append(jnp.where(is_both, owner[0] * 4, owner[1 + step] * 4 + 2 + step))
    scalars = jnp.where(lanes == 0, jnp.where(fits, 1, 0), 0)
    numbers = []
    for index in range(3):
        mine = own_kind[index] & (handler[index] == rep)
        numbers.append(jnp.sum(jnp.where(mine, lanes.astype(F32), 0.0)).astype(jnp.int32))
        spot = jnp.max(jnp.where(mine, own_place[index] // n_rep, 0), axis=1, keepdims=True)
        scalars = jnp.where(lanes == 4 + index, spot, scalars)
    for step in range(STEPS):
        amount = (total[step] - rep + n_rep - 1) // n_rep
        scalars = jnp.where(lanes == 7 + step, amount, scalars)
    amount = (both_end - rep + n_rep - 1) // n_rep
    scalars = jnp.where(lanes == 9, amount, scalars)
    moved = own_kind[0] | own_kind[1]
    moved_amount = jnp.sum(jnp.where(moved, 1, 0), axis=1, keepdims=True)
    scalars = jnp.where(lanes == 10, moved_amount, scalars)
    moved_rank = (own_rank[0] + own_rank[1]).astype(jnp.int32)
    spots = jnp.where(moved, moved_rank, moved_amount + lanes - moved_rank)
    listed = (prep_width // BLOCK) * 8
    numbers_down = lax.broadcasted_iota(jnp.int32, (listed, BLOCK), 0)
    spots_down = jnp.sum(jnp.where(numbers_down == lanes, spots, 0), axis=1, keepdims=True)
    members = jnp.sum(jnp.where(spots_down == lanes, numbers_down, 0), axis=0, keepdims=True)
    gap = jnp.zeros((1, BLOCK), jnp.int32)
    rows = [home[0], home[1], scalars, places[0], places[1], spots, members, gap]
    table_ref[...] = jnp.concatenate(rows, axis=0)
    return numbers


def share_kernel(n_blk, n_rep, list_ref, count_ref, kin_ref, der_ref, last_ref, table_ref, out_ref):
    numbers = share_blocks(n_blk, n_rep, list_ref, count_ref, table_ref)
    where = [block_at(number) for number in numbers]
    gap = jnp.zeros((2, BLOCK), F32)
    rows = [
        predicted_block(kin_ref, der_ref, last_ref, where[0], 0.0),
        0.0 - last_ref[:, where[0]],
        gap[0:1],
        der_ref[:, where[0]],
        gap,
        predicted_block(kin_ref, der_ref, last_ref, where[1], 0.0),
        gap,
        predicted_block(kin_ref, der_ref, last_ref, where[2], step_length),
        gap,
    ]
    mine = jnp.concatenate(rows, axis=0)
    for other in range(n_blk):
        out_ref[other] = mine


def write_part(n_blk, width, stars, mass, where, piece_ref, moment_ref):
    piece_ref[where, :] = source_pieces(stars).T.astype(BF16)
    ones = jnp.ones((1, prep_width), F32)
    moments = jnp.concatenate([stars, ones, jnp.zeros_like(ones)], axis=0) * (mass / (width * n_blk))
    moments = jnp.concatenate([stack_three(moments), jnp.zeros((8, prep_width), F32)], axis=0)
    moment_ref[:, where] = moments.astype(BF16)


def write_pieces(n_blk, kin_ref, der_ref, last_ref, mass_ref, pred_ref, piece_ref, moment_ref):
    width = kin_ref.shape[1]
    total = jnp.zeros((6, prep_width), F32)
    for part in range(width // prep_width):
        where = pl.ds(part * prep_width, prep_width)
        stars = predicted_block(kin_ref, der_ref, last_ref, where, 0.0)
        pred_ref[:, where] = stars
        total = total + stars
    centre = jnp.sum(total, axis=1, keepdims=True) / width
    for part in range(width // prep_width):
        where = pl.ds(part * prep_width, prep_width)
        stars = pred_ref[:, where] - centre
        write_part(n_blk, width, stars, mass_ref[:, where], where, piece_ref, moment_ref)
    return centre


def write_listed(
    n_blk, parts, table_ref, centre, kin_ref, der_ref, last_ref, mass_ref, piece_ref, moment_ref
):
    blocks = prep_width // BLOCK
    for part in parts:
        places = [block_at(table_ref[6, part * blocks + index]) for index in range(blocks)]
        stars = [predicted_block(kin_ref, der_ref, last_ref, one, step_length) for one in places]
        stars = jnp.concatenate([one - centre for one in stars], axis=1)
        mass = jnp.concatenate([mass_ref[:, one] for one in places], axis=1)
        where = pl.ds(part * prep_width, prep_width)
        write_part(n_blk, kin_ref.shape[1], stars, mass, where, piece_ref, moment_ref)


def block_forces(blocks, parts, piece_ref, moment_ref):
    against = [target_pieces(stars) for stars in blocks]
    order = [(index, part) for index in range(len(blocks)) for part in parts]
    by_weight = [jnp.zeros((32, 2 * BLOCK), F32) for stars in blocks]
    by_radial = [jnp.zeros((32, 2 * BLOCK), F32) for stars in blocks]

    def meet(index, part):
        where = pl.ds(part * ahead_chunk, ahead_chunk)
        return jnp.dot(piece_ref[where, :], against[index], preferred_element_type=F32)

    def halves(value):
        high = value.astype(BF16)
        low = (value - high.astype(F32)).astype(BF16)
        return jnp.concatenate([high, low], axis=1)

    both = meet(*order[0])
    for turn, (index, part) in enumerate(order):
        ahead = meet(*order[turn + 1]) if turn + 1 < len(order) else None
        inverse = lax.rsqrt(both[:, :BLOCK])
        inverse_sq = inverse * inverse
        weight = inverse * inverse_sq
        radial = weight * (inverse_sq * both[:, BLOCK:])
        moments = moment_ref[:, pl.ds(part * ahead_chunk, ahead_chunk)]
        by_weight[index] += jnp.dot(moments, halves(weight), preferred_element_type=F32)
        by_radial[index] += jnp.dot(moments, halves(radial), preferred_element_type=F32)
        both = ahead

    def gather_up(value):
        value = value[0:8] + value[8:16] + value[16:24]
        return value[:, :BLOCK] + value[:, BLOCK:]

    results = []
    for index, stars in enumerate(blocks):
        on_weight, on_radial = gather_up(by_weight[index]), gather_up(by_radial[index])
        sums = on_weight[0:6] - stars * on_weight[6:7]
        pull = on_radial[0:3] - stars[0:3] * on_radial[6:7]
        gap = jnp.zeros((ROWS - 6, BLOCK), F32)
        results.append(jnp.concatenate([sums[0:3], sums[3:6] - 3.0 * pull, gap], axis=0))
    return results


def all_forces(begin, end, parts, stars_of, store, piece_ref, moment_ref):
    def some(first, size):
        blocks = [stars_of(first + index) for index in range(size)]
        results = block_forces(blocks, parts, piece_ref, moment_ref)
        for index, result in enumerate(results):
            store(first + index, result)

    pairs = (end - begin) // 2

    def two(pair, carry):
        some(begin + pair * 2, 2)
        return carry

    lax.fori_loop(0, pairs, two, 0)

    @pl.when(end > begin + pairs * 2)
    def _():
        some(begin + pairs * 2, 1)


def every_part(piece_ref):
    return list(range(piece_ref.shape[0] // ahead_chunk))


def pieces_kernel(
    n_blk, kin_ref, der_ref, last_ref, mass_ref, piece_ref, moment_ref, centre_ref, pred_ref
):
    centre = write_pieces(
        n_blk, kin_ref, der_ref, last_ref, mass_ref, pred_ref, piece_ref, moment_ref
    )
    centre_ref[...] = jnp.broadcast_to(centre, (6, BLOCK))


def early_parts():
    return early_chunks * ahead_chunk // prep_width


def early_pieces_kernel(
    n_blk, table_ref, kin_ref, der_ref, last_ref, mass_ref, centre_ref, piece_ref, moment_ref
):
    centre = centre_ref[...]
    parts = range(early_parts(), kin_ref.shape[1] // prep_width)
    piece_ref[pl.ds(0, early_chunks * ahead_chunk), :] = jnp.zeros(
        (early_chunks * ahead_chunk, piece_rows), BF16
    )
    moment_ref[:, pl.ds(0, early_chunks * ahead_chunk)] = jnp.zeros(
        (32, early_chunks * ahead_chunk), BF16
    )
    write_listed(
        n_blk, parts, table_ref, centre, kin_ref, der_ref, last_ref, mass_ref, piece_ref, moment_ref
    )


def late_chunks(table_ref, chunks):
    needed = (table_ref[2, 10] * BLOCK + ahead_chunk - 1) // ahead_chunk
    return jnp.minimum(jnp.maximum(needed, early_chunks), chunks)


def early_forces_kernel(
    turn, table_ref, after_ref, target_ref, piece_ref, moment_ref, centre_ref, out_ref, *more_refs
):
    out_ref[...] = jnp.zeros_like(out_ref)
    last = turn == 2
    if last:
        write_next_targets(table_ref, after_ref, target_ref, more_refs[0])
        target_ref = more_refs[0]
    else:
        for zero_ref in more_refs:
            zero_ref[...] = jnp.zeros_like(zero_ref)
    moved_end, end = table_ref[2, 9], table_ref[2, 8]
    begin = jnp.minimum(moved_end + turn * early_pair, end)

    def number(index):
        if not last:
            return begin + index
        return jnp.where(index < end - begin, begin + index, index - (end - begin))

    def stars_of(index):
        place = number(index) if last else table_ref[4, number(index)]
        return target_ref[place][0:6] - centre_ref[...]

    def store(index, result):
        out_ref[number(index)] = result

    amount = end - begin + moved_end if last else jnp.minimum(early_pair, end - begin)

    parts = every_part(piece_ref)
    late = late_chunks(table_ref, len(parts))

    for split in range(early_chunks, len(parts)):

        @pl.when(late == split)
        def _(split=split):
            all_forces(0, amount, parts[split:], stars_of, store, piece_ref, moment_ref)


def first_forces_kernel(table_ref, target_ref, piece_ref, moment_ref, centre_ref, out_ref):
    out_ref[...] = jnp.zeros_like(out_ref)

    def stars_of(index):
        return target_ref[table_ref[3, index]][0:6] - centre_ref[...]

    def store(index, result):
        out_ref[index] = result

    all_forces(0, table_ref[2, 7], every_part(piece_ref), stars_of, store, piece_ref, moment_ref)


def flag_rows():
    rows = lax.broadcasted_iota(jnp.int32, (CAP * ROWS, BLOCK), 0)
    return jnp.bitwise_and(rows, ROWS - 1) == 6


def flagged_total_kernel(n_blk, n_rep, part_ref, out_ref):
    total = part_ref[0]
    for other in range(1, n_blk):
        total = total + part_ref[other]
    total = jnp.where(flag_rows(), 1.0, total)
    for other in range(n_rep):
        out_ref[other] = total


def middle_kernel(
    n_rep, table_ref, term_a, term_b, term_c, term_d, early_ref, share_ref, force_ref
):
    force_ref[...] = term_a[...] + ((term_b[...] + term_c[...]) + term_d[...])
    own = jnp.concatenate([force_ref[table_ref[2, 4]], force_ref[table_ref[2, 5]]], axis=0)
    own = jnp.where(flag_rows(), 1.0, own)
    for other in range(n_rep):
        share_ref[other] = own


def write_next_targets(table_ref, force_ref, target_ref, next_ref):
    def one(index, carry):
        place = table_ref[4, index]
        is_both = index < table_ref[2, 9]

        @pl.when(is_both)
        def _():
            head, deriv = target_ref[place], target_ref[place + 1][0:6]
            forces = force_ref[index][0:6]
            moved = correct(head[0:6], deriv, forces, head[6:7])
            ahead = predict(moved[:3], moved[3:], forces[:3], forces[3:], step_length)
            next_ref[index] = jnp.concatenate([ahead, head[6:8]], axis=0)

        @pl.when(jnp.logical_not(is_both))
        def _():
            next_ref[index] = target_ref[place]

        return carry

    lax.fori_loop(0, table_ref[2, 8], one, 0)


def place_forces(step, table_ref, force_ref, placed_ref):
    for number in range(placed_ref.shape[1] // BLOCK):
        code = table_ref[step, number]
        tile = force_ref[jnp.maximum(code, 0)]
        tile = tile * jnp.where(code >= 0, 1.0, 0.0)
        placed_ref[:, pl.ds(number * BLOCK, BLOCK)] = tile


def moved_part(step, where, placed_ref, kin_ref, der_ref, last_ref):
    time_now = step * step_length
    placed = placed_ref[:, where]
    forces, moved = placed[0:6], placed[6:7] > 0.5
    kin, der, last = kin_ref[:, where], der_ref[:, where], last_ref[:, where]
    interval = time_now - last
    predicted = predict(kin[:3], kin[3:], der[:3], der[3:], interval)
    corrected = correct(predicted, der, forces, interval)
    return (
        jnp.where(moved, corrected, kin),
        jnp.where(moved, forces, der),
        jnp.where(moved, time_now, last),
    )


def second_forces_kernel(
    n_blk, table_ref, force_ref, target_ref, early_a, early_b, early_c, centre_ref,
    kin_ref, der_ref, last_ref, mass_ref,
    out_ref, new_kin_ref, new_der_ref, new_last_ref, placed_ref, piece_ref, moment_ref,
):
    width = kin_ref.shape[1]
    place_forces(0, table_ref, force_ref, placed_ref)
    for part in range(width // prep_width):
        where = pl.ds(part * prep_width, prep_width)
        kin, der, last = moved_part(0, where, placed_ref, kin_ref, der_ref, last_ref)
        new_kin_ref[:, where] = kin
        new_der_ref[:, where] = der
        new_last_ref[:, where] = last
    centre = centre_ref[...]
    parts = every_part(piece_ref)
    late = late_chunks(table_ref, len(parts))
    steps = ahead_chunk // prep_width

    def listed(parts):
        write_listed(
            n_blk, parts, table_ref, centre, new_kin_ref, new_der_ref, new_last_ref, mass_ref,
            piece_ref, moment_ref,
        )

    listed(range(early_parts()))

    for more in range(early_chunks, len(parts)):

        @pl.when(late > more)
        def _(more=more):
            listed(range(more * steps, (more + 1) * steps))

    out_ref[...] = jnp.zeros_like(out_ref)

    def stars_of(index):
        return target_ref[index][0:6] - centre

    def store(index, result):
        place = table_ref[4, index]
        early = (early_a[index] + early_b[index]) + early_c[index]
        out_ref[(place // 4) * 2 + place % 2] = result + early

    for split in range(early_chunks, len(parts) + 1):

        @pl.when(late == split)
        def _(split=split):
            all_forces(0, table_ref[2, 8], parts[:split], stars_of, store, piece_ref, moment_ref)


def last_kernel(
    table_ref, force_ref, kin_ref, der_ref, last_ref, new_kin_ref, new_der_ref, placed_ref
):
    place_forces(1, table_ref, force_ref, placed_ref)
    for part in range(kin_ref.shape[1] // prep_width):
        where = pl.ds(part * prep_width, prep_width)
        kin, der, last = moved_part(1, where, placed_ref, kin_ref, der_ref, last_ref)
        new_kin_ref[:, where] = kin
        new_der_ref[:, where] = der


def shape_of(*sizes):
    return jax.ShapeDtypeStruct(sizes, F32)


def run_kernel(body, scalars, arrays, out_shape, scratch=(), after=None):
    scalar_specs = [pl.BlockSpec(memory_space=pltpu.SMEM)] * len(scalars)
    if after is not None:
        arrays = [after, *arrays]
    return pl.pallas_call(
        body,
        out_shape=out_shape,
        in_specs=scalar_specs
        + [pl.BlockSpec(memory_space=pltpu.VMEM)] * len(arrays),
        out_specs=jax.tree.map(lambda leaf: pl.BlockSpec(memory_space=pltpu.VMEM), out_shape),
        scratch_shapes=list(scratch),
        compiler_params=pltpu.CompilerParams(vmem_limit_bytes=32 * 2**20),
    )(*scalars, *arrays)


def plain_steps(kinematics, derivatives, mass, last, block_list, block_count):
    width = kinematics.shape[1]
    n_blk = lax.axis_size("blk")
    n_rep = lax.axis_size("rep")
    flat_list = block_list.reshape(-1)
    flat_count = block_count.reshape(-1)
    targets = run_kernel(
        functools.partial(targets_kernel, 0, n_blk, n_rep),
        [flat_list],
        [kinematics, derivatives, last],
        shape_of(n_blk, CAP * ROWS, BLOCK),
    )
    for step in range(STEPS):
        gathered = lax.all_to_all(targets, "blk", 0, 0, tiled=True)
        partial_forces = run_kernel(
            functools.partial(forces_kernel, step, n_blk, n_rep),
            [flat_count],
            [gathered.reshape(n_blk * CAP, ROWS, BLOCK), kinematics, derivatives, last, mass],
            shape_of(n_blk * CAP, ROWS, BLOCK),
            [
                pltpu.VMEM((6, width), F32),
                pltpu.VMEM((width, piece_rows), BF16),
                pltpu.VMEM((32, width), BF16),
            ],
        )
        partial_forces = partial_forces.reshape(n_blk, CAP * ROWS, BLOCK)
        spread = lax.all_to_all(partial_forces, "blk", 0, 0, tiled=True)
        mine = run_kernel(
            functools.partial(total_kernel, n_blk, n_rep),
            [],
            [spread],
            shape_of(n_rep, CAP * ROWS, BLOCK),
        )
        forces = lax.all_to_all(mine, "rep", 0, 0, tiled=True)
        out_shape = [shape_of(6, width), shape_of(6, width), shape_of(1, width)]
        if step + 1 < STEPS:
            out_shape.append(shape_of(n_blk, CAP * ROWS, BLOCK))
        kinematics, derivatives, last, *rest = run_kernel(
            functools.partial(update_kernel, step, n_blk, n_rep),
            [flat_list, flat_count],
            [forces.reshape(n_rep * CAP, ROWS, BLOCK), kinematics, derivatives, last],
            out_shape,
        )
        if rest:
            targets = rest[0]
    return (kinematics, derivatives)


def from_partner(value, distance):
    n_blk = lax.axis_size("blk")
    return lax.ppermute(value, "blk", [(i, i ^ distance) for i in range(n_blk)])


def shared_steps(kinematics, derivatives, mass, last, table, gathered, pieces, early_pieces):
    width = kinematics.shape[1]
    n_blk = lax.axis_size("blk")
    n_rep = lax.axis_size("rep")
    piece_scratch = [pltpu.VMEM((width, piece_rows), BF16), pltpu.VMEM((32, width), BF16)]
    partial_forces = run_kernel(
        first_forces_kernel,
        [table],
        [gathered, *pieces],
        shape_of(first_slots, ROWS, BLOCK),
    )
    value = partial_forces.reshape(first_slots * ROWS, BLOCK)
    value = value + from_partner(value, 1)

    def early_forces(turn, after, *more):
        return run_kernel(
            functools.partial(early_forces_kernel, turn),
            [table],
            [gathered, *early_pieces, pieces[2]],
            [shape_of(n_rep, ROWS, BLOCK), *more],
            after=after,
        )

    first_early, zero = early_forces(0, value, shape_of(first_slots * ROWS, BLOCK))
    value = (value + from_partner(value, 2)) + zero
    early = [first_early, *early_forces(1, value)]
    terms = [value] + [from_partner(value, distance) for distance in (4, 12, 8)]
    terms = [term.reshape(first_slots, ROWS, BLOCK) for term in terms]
    shares, forces = run_kernel(
        functools.partial(middle_kernel, n_rep),
        [table],
        [*terms, early[1]],
        [shape_of(n_rep, 2 * ROWS, BLOCK), shape_of(first_slots, ROWS, BLOCK)],
    )
    last_early, targets = early_forces(2, forces, shape_of(n_rep, ROWS, BLOCK))
    early.append(last_early)
    shares = lax.all_to_all(shares, "rep", 0, 0, tiled=True)
    shard = [kinematics, derivatives, last, mass]
    partial_forces, kinematics, derivatives, last = run_kernel(
        functools.partial(second_forces_kernel, n_blk),
        [table],
        [shares.reshape(n_rep * 2, ROWS, BLOCK), targets, *early, pieces[2], *shard],
        [shape_of(n_blk * 2, ROWS, BLOCK), shape_of(6, width), shape_of(6, width), shape_of(1, width)],
        [pltpu.VMEM((ROWS, width), F32)] + piece_scratch,
    )
    spread = lax.all_to_all(
        partial_forces.reshape(n_blk, 2 * ROWS, BLOCK), "blk", 0, 0, tiled=True
    )
    mine = run_kernel(
        functools.partial(flagged_total_kernel, n_blk, n_rep),
        [],
        [spread],
        shape_of(n_rep, 2 * ROWS, BLOCK),
    )
    shares = lax.all_to_all(mine, "rep", 0, 0, tiled=True)
    return run_kernel(
        last_kernel,
        [table],
        [shares.reshape(n_rep * 2, ROWS, BLOCK), kinematics, derivatives, last],
        [shape_of(6, width), shape_of(6, width)],
        [pltpu.VMEM((ROWS, width), F32)],
    )


def per_device(kinematics, derivatives, masses, last_time, block_list, block_count):
    width = kinematics.shape[1]
    n_blk = lax.axis_size("blk")
    n_rep = lax.axis_size("rep")
    mass = masses.reshape(1, width)
    last = last_time.reshape(1, width)
    table, targets = run_kernel(
        functools.partial(share_kernel, n_blk, n_rep),
        [],
        [block_list.transpose(0, 1, 3, 2), block_count, kinematics, derivatives, last],
        [jax.ShapeDtypeStruct((8, BLOCK), jnp.int32), shape_of(n_blk, 4 * ROWS, BLOCK)],
    )
    gathered = lax.all_to_all(targets, "blk", 0, 0, tiled=True)
    gathered = gathered.reshape(n_blk * 4, ROWS, BLOCK)
    piece_shapes = [
        jax.ShapeDtypeStruct((width, piece_rows), BF16),
        jax.ShapeDtypeStruct((32, width), BF16),
        shape_of(6, BLOCK),
    ]
    shard = [kinematics, derivatives, last, mass]
    pieces = run_kernel(
        functools.partial(pieces_kernel, n_blk),
        [],
        shard,
        piece_shapes,
        [pltpu.VMEM((6, width), F32)],
    )
    early_pieces = run_kernel(
        functools.partial(early_pieces_kernel, n_blk),
        [table],
        [*shard, pieces[2]],
        piece_shapes[:2],
    )
    return tuple(
        lax.cond(
            table[2, 0] > 0,
            lambda: tuple(
                shared_steps(
                    kinematics, derivatives, mass, last, table, gathered, pieces, early_pieces
                )
            ),
            lambda: tuple(
                plain_steps(kinematics, derivatives, mass, last, block_list, block_count)
            ),
        )
    )


def solution(mesh):
    return jax.shard_map(
        per_device,
        mesh=mesh,
        in_specs=(P(None, "blk"), P(None, "blk"), P("blk"), P("blk"), P(), P()),
        out_specs=(P(None, "blk"), P(None, "blk")),
        check_vma=False,
    )
```

profile of v0, /device:TPU:32, one launch (start us, length us, event | category | flops | bytes accessed | tf_op | source)
XLA Modules:
  0.0 97.7 jit_solution(11547999473727739872)
XLA Ops:
  0.6 2.4 %shard_map.77 = (s32[8,128]{1,0:T(8,128)S(1)}, f32[16,32,128]{2,1,0:T(8,128)}) custom-call(s32[2,16,2,16]{3,2,1,0:T(2,128)} %bitcast.49, s32[2,16,16]{2,1,0:T(8,128)} %count_ref.1, f32[6,4096]{1,0:T(8,128)} %kin_ref.5, f32[6,4096]{1,0:T(8,128)} %der_ref.5, f32[1,4096]{1,0:T(1,128)} %bitcast.40), custom_call_target="tpu_custom_call" | custom-call | tf_op jit(solution)/shard_map/pallas_call | solution.py:688
  3.0 0.0 copy-start
  3.0 0.0 copy-start.1
  3.0 0.0 copy-start.2
  3.0 0.0 copy-start.3
  3.0 5.6 %all-to-all-start.9 = ((f32[16,32,128]{2,1,0:T(8,128)}), f32[16,32,128]{2,1,0:T(8,128)S(1)}, u32[]{:S(2)}, u32[]{:S(2)}) async-start(f32[16,32,128]{2,1,0:T(8,128)} %get-tuple-element.78), calls=%async_computation.9 | async-start | bytes 524288 | tf_op jit(solution)/shard_map/all_to_all | solution.py:828
  8.6 0.0 copy-done
  8.6 0.0 copy-done.1
  8.6 0.0 copy-done.2
  8.6 0.0 copy-done.3
  8.6 0.9 shard_map.78
  9.5 0.5 slice.3
  10.7 0.0 copy-start.4
  10.7 0.0 copy-start.5
  10.7 1.1 %shard_map.79 = (bf16[4096,128]{1,0:T(8,128)(2,1)S(1)}, bf16[32,4096]{1,0:T(8,128)(2,1)S(1)}) custom-call(s32[8,128]{1,0:T(8,128)S(1)} %get-tuple-element.77.table_ref, f32[6,4096]{1,0:T(8,128)S(1)} %copy-done, f32[6,4096]{1,0:T(8,128)S(1)} %copy-done.1, f32[1,4096]{1,0:T(1,128)S(1)} %bitcast.42, f32[1,4096]{1,0:T(1,128)S(1)} %bitcast.46, ...), custom_call_target="tpu_custom_call" | custom-call | tf_op jit(solution)/shard_map/pallas_call | solution.py:688
  11.7 4.5 %all-to-all-done.9 = f32[16,32,128]{2,1,0:T(8,128)S(1)} async-done(((f32[16,32,128]{2,1,0:T(8,128)}), f32[16,32,128]{2,1,0:T(8,128)S(1)}, u32[]{:S(2)}, u32[]{:S(2)}) %all-to-all-start.9) | async-done | bytes 262176 | tf_op jit(solution)/shard_map/all_to_all | solution.py:828
  16.3 0.0 copy-done.4
  16.3 0.0 copy-done.5
  16.3 81.4 %conditional.1 = ((f32[6,4096]{1,0:T(8,128)}, f32[6,4096]{1,0:T(8,128)})) conditional(s32[]{:T(128)} %bitcast.17, (s32[2,16,16,2]{2,3,1,0:T(2,128)S(1)}, s32[2,16,16]{2,1,0:T(8,128)S(1)}, f32[6,4096]{1,0:T(8,128)S(1)}, f32[6,4096]{1,0:T(8,128)S(1)}, f32[1,4096]{1,0:T(1,128)S(1)}, /*index=5*/f32[1,4096]{1,0:T(1,128)S(1)}) %tuple.30, ...), branch_computations={%region_0.0_spmd, %region_1.0_spmd} | conditional | flops 36864 | bytes 2244848 | solution.py:850
  16.3 13.0 %branch_1_fun.8 = f32[12,8,128]{2,1,0:T(8,128)S(1)} custom-call(s32[8,128]{1,0:T(8,128)S(1)} %get-tuple-element.47.table_ref, f32[64,8,128]{2,1,0:T(8,128)S(1)} %bitcast.36, bf16[4096,128]{1,0:T(8,128)(2,1)S(1)} %get-tuple-element.49.piece_ref, bf16[32,4096]{1,0:T(8,128)(2,1)S(1)} %get-tuple-element.50.moment_ref, f32[6,128]{1,0:T(8,128)S(1)} %get-tuple-element.51.centre_ref), custom_call_target="tpu_custom_call" | custom-call | tf_op jit(solution)/shard_map/cond/branch_1_fun/pallas_call | solution.py:688
  29.3 0.4 collective-permute-start
  29.7 1.1 %collective-permute-done = f32[96,128]{1,0:T(8,128)S(1)} collective-permute-done((f32[96,128]{1,0:T(8,128)S(1)}, f32[96,128]{1,0:T(8,128)S(1)}, u32[]{:S(2)}, u32[]{:S(2)}) %collective-permute-start) | collective-permute-done | bytes 49184 | tf_op jit(solution)/shard_map/cond/branch_1_fun/ppermute | solution.py:749
  30.8 0.8 collective-permute-start.1
  31.6 2.0 %branch_1_fun.9 = (f32[16,8,128]{2,1,0:T(8,128)S(1)}, f32[96,128]{1,0:T(8,128)S(1)}) custom-call(s32[8,128]{1,0:T(8,128)S(1)} %get-tuple-element.47.table_ref, f32[96,128]{1,0:T(8,128)S(1)} %bitcast_add_fusion.after_ref, f32[64,8,128]{2,1,0:T(8,128)S(1)} %bitcast.37, bf16[4096,128]{1,0:T(8,128)(2,1)S(1)} %get-tuple-element.52.piece_ref, ...), custom_call_target="tpu_custom_call" | custom-call | tf_op jit(solution)/shard_map/cond/branch_1_fun/pallas_call | solution.py:688
  33.6 1.3 %collective-permute-done.1 = f32[96,128]{1,0:T(8,128)S(1)} collective-permute-done((f32[96,128]{1,0:T(8,128)S(1)}, f32[96,128]{1,0:T(8,128)S(1)}, u32[]{:S(2)}, u32[]{:S(2)}) %collective-permute-start.1) | collective-permute-done | bytes 49184 | tf_op jit(solution)/shard_map/cond/branch_1_fun/ppermute | solution.py:749
  35.0 1.3 %collective-permute-start.4 = (f32[96,128]{1,0:T(8,128)S(1)}, f32[96,128]{1,0:T(8,128)S(1)}, u32[]{:S(2)}, u32[]{:S(2)}) collective-permute-start(f32[96,128]{1,0:T(8,128)S(1)} %add_add_fusion.after_ref), channel_id=1, source_target_pairs={{0,128},{16,144},{32,160},{48,176},{64,192},{80,208},{96,224},{112... | collective-permute-start | bytes 147464 | tf_op jit(solution)/shard_map/cond/branch_1_fun/ppermute | solution.py:749
  36.3 1.5 %collective-permute-start.3 = (f32[96,128]{1,0:T(8,128)S(1)}, f32[96,128]{1,0:T(8,128)S(1)}, u32[]{:S(2)}, u32[]{:S(2)}) collective-permute-start(f32[96,128]{1,0:T(8,128)S(1)} %add_add_fusion.after_ref), channel_id=1, source_target_pairs={{0,192},{16,208},{32,224},{48,240},{64,128},{80,144},{96,160},{112... | collective-permute-start | bytes 147464 | tf_op jit(solution)/shard_map/cond/branch_1_fun/ppermute | solution.py:749
  37.7 0.8 collective-permute-start.2
  38.5 2.0 %branch_1_fun.10.early_ref.early_b = f32[16,8,128]{2,1,0:T(8,128)S(1)} custom-call(s32[8,128]{1,0:T(8,128)S(1)} %get-tuple-element.47.table_ref, f32[96,128]{1,0:T(8,128)S(1)} %add_add_fusion.after_ref, f32[64,8,128]{2,1,0:T(8,128)S(1)} %bitcast.38, bf16[4096,128]{1,0:T(8,128)(2,1)S(1)} %get-tuple-element.52.piece_ref, ...), custom_call_target="tpu_custom_call" | custom-call | tf_op jit(solution)/shard_map/cond/branch_1_fun/pallas_call | solution.py:688
  40.6 0.7 collective-permute-done.4
  41.2 0.4 collective-permute-done.3
  41.6 0.2 collective-permute-done.2
  41.8 1.3 %branch_1_fun.11 = (f32[16,16,128]{2,1,0:T(8,128)}, f32[12,8,128]{2,1,0:T(8,128)S(1)}) custom-call(s32[8,128]{1,0:T(8,128)S(1)} %get-tuple-element.47.table_ref, f32[12,8,128]{2,1,0:T(8,128)S(1)} %bitcast.30, f32[12,8,128]{2,1,0:T(8,128)S(1)} %bitcast.35, f32[12,8,128]{2,1,0:T(8,128)S(1)} %bitcast.34, f32[12,8,128]{2,1,0:T(8,128)S(1)} %bitcast.33, ...), custom_call_target="tpu_custom_call" | custom-call | tf_op jit(solution)/shard_map/cond/branch_1_fun/pallas_call | solution.py:688
  43.1 10.9 %all-to-all-start.6 = ((f32[16,16,128]{2,1,0:T(8,128)}), f32[16,16,128]{2,1,0:T(8,128)S(1)}, u32[]{:S(2)}, u32[]{:S(2)}) async-start(f32[16,16,128]{2,1,0:T(8,128)} %get-tuple-element.55), calls=%async_computation.6 | async-start | bytes 262144 | tf_op jit(solution)/shard_map/cond/branch_1_fun/all_to_all | solution.py:788
  54.0 5.7 %branch_1_fun.12 = (f32[16,8,128]{2,1,0:T(8,128)S(1)}, f32[16,8,128]{2,1,0:T(8,128)S(1)}) custom-call(s32[8,128]{1,0:T(8,128)S(1)} %get-tuple-element.47.table_ref, f32[12,8,128]{2,1,0:T(8,128)S(1)} %get-tuple-element.56.after_ref, f32[64,8,128]{2,1,0:T(8,128)S(1)} %bitcast.39, bf16[4096,128]{1,0:T(8,128)(2,1)S(1)} %get-tuple-element.52.piece_ref, ...), custom_call_target="tpu_custom_call" | custom-call | tf_op jit(solution)/shard_map/cond/branch_1_fun/pallas_call | solution.py:688
  59.8 3.8 %all-to-all-done.6 = f32[16,16,128]{2,1,0:T(8,128)S(1)} async-done(((f32[16,16,128]{2,1,0:T(8,128)}), f32[16,16,128]{2,1,0:T(8,128)S(1)}, u32[]{:S(2)}, u32[]{:S(2)}) %all-to-all-start.6) | async-done | bytes 131104 | tf_op jit(solution)/shard_map/cond/branch_1_fun/all_to_all | solution.py:788
  63.6 9.1 %branch_1_fun.13 = (f32[32,8,128]{2,1,0:T(8,128)S(1)}, f32[6,4096]{1,0:T(8,128)S(1)}, f32[6,4096]{1,0:T(8,128)S(1)}, f32[1,4096]{1,0:T(1,128)S(1)}) custom-call(s32[8,128]{1,0:T(8,128)S(1)} %get-tuple-element.47.table_ref, f32[32,8,128]{2,1,0:T(8,128)S(1)} %bitcast.29, f32[16,8,128]{2,1,0:T(8,128)S(1)} %get-tuple-element.57.target_ref, ...), custom_call_target="tpu_custom_call" | custom-call | tf_op jit(solution)/shard_map/cond/branch_1_fun/pallas_call | solution.py:688
  72.6 9.4 %all_to_all.46.part_ref = f32[16,16,128]{2,1,0:T(8,128)S(1)} all-to-all(f32[16,16,128]{2,1,0:T(8,128)S(1)} %bitcast.32), channel_id=1, replica_groups=mesh['blk'=16,'rep'=16] {'blk'}, dimensions={0} | all-to-all | bytes 262144 | tf_op jit(solution)/shard_map/cond/branch_1_fun/all_to_all | solution.py:797
  82.1 14.1 %all_to_all.47 = f32[16,16,128]{2,1,0:T(8,128)S(1)} all-to-all(f32[16,16,128]{2,1,0:T(8,128)S(1)} %branch_1_fun.14), channel_id=1, replica_groups=mesh['blk'=16,'rep'=16] {'rep'}, dimensions={0} | all-to-all | bytes 262144 | tf_op jit(solution)/shard_map/cond/branch_1_fun/all_to_all | solution.py:806
  96.1 1.5 %branch_1_fun.15 = (f32[6,4096]{1,0:T(8,128)}, f32[6,4096]{1,0:T(8,128)}) custom-call(s32[8,128]{1,0:T(8,128)S(1)} %get-tuple-element.47.table_ref, f32[32,8,128]{2,1,0:T(8,128)S(1)} %bitcast.24, f32[6,4096]{1,0:T(8,128)S(1)} %get-tuple-element.65.kin_ref, f32[6,4096]{1,0:T(8,128)S(1)} %get-tuple-element.66.der_ref, f32[1,4096]{1,0:T(1,128)S(1)} %get-tuple-element.67.last_ref), custom_call_target="tpu_custom_call" | custom-call | tf_op jit(solution)/shard_map/cond/branch_1_fun/pallas_call | solution.py:688
  (3 shorter events, 0.0 us)
Async XLA Ops:
  3.0 5.6 %copy-start = (f32[6,4096]{1,0:T(8,128)S(1)}, f32[6,4096]{1,0:T(8,128)}, u32[]{:S(2)}) copy-start(f32[6,4096]{1,0:T(8,128)} %kin_ref.5) | copy-start | bytes 294916
  3.0 5.6 %copy-start.1 = (f32[6,4096]{1,0:T(8,128)S(1)}, f32[6,4096]{1,0:T(8,128)}, u32[]{:S(2)}) copy-start(f32[6,4096]{1,0:T(8,128)} %der_ref.5) | copy-start | bytes 294916
  3.0 5.6 %copy-start.2 = (f32[4096]{0:T(1024)S(1)}, f32[4096]{0:T(1024)}, u32[]{:S(2)}) copy-start(f32[4096]{0:T(1024)} %param.11) | copy-start | bytes 49156
  3.0 5.6 %copy-start.3 = (f32[4096]{0:T(1024)S(1)}, f32[4096]{0:T(1024)}, u32[]{:S(2)}) copy-start(f32[4096]{0:T(1024)} %param.10) | copy-start | bytes 49156
  3.0 13.3 %all-to-all-start.9 = ((f32[16,32,128]{2,1,0:T(8,128)}), f32[16,32,128]{2,1,0:T(8,128)S(1)}, u32[]{:S(2)}, u32[]{:S(2)}) async-start(f32[16,32,128]{2,1,0:T(8,128)} %get-tuple-element.78), calls=%async_computation.9 | async-start | bytes 524288 | tf_op jit(solution)/shard_map/all_to_all | solution.py:828
  10.7 5.6 %copy-start.4 = (s32[2,16,16,2]{2,3,1,0:T(2,128)S(1)}, s32[2,16,16,2]{2,3,1,0:T(2,128)}, u32[]{:S(2)}) copy-start(s32[2,16,16,2]{2,3,1,0:T(2,128)} %param.12) | copy-start | bytes 12292
  10.7 5.6 %copy-start.5 = (s32[2,16,16]{2,1,0:T(8,128)S(1)}, s32[2,16,16]{2,1,0:T(8,128)}, u32[]{:S(2)}) copy-start(s32[2,16,16]{2,1,0:T(8,128)} %count_ref.1) | copy-start | bytes 6148
  29.3 1.5 %collective-permute-start = (f32[96,128]{1,0:T(8,128)S(1)}, f32[96,128]{1,0:T(8,128)S(1)}, u32[]{:S(2)}, u32[]{:S(2)}) collective-permute-start(f32[96,128]{1,0:T(8,128)S(1)} %bitcast.31), channel_id=1, source_target_pairs={{0,16},{16,0},{32,48},{48,32},{64,80},{80,64},{96,112},{112,96},{1... | collective-permute-start | bytes 147464 | tf_op jit(solution)/shard_map/cond/branch_1_fun/ppermute | solution.py:749
  30.8 4.2 %collective-permute-start.1 = (f32[96,128]{1,0:T(8,128)S(1)}, f32[96,128]{1,0:T(8,128)S(1)}, u32[]{:S(2)}, u32[]{:S(2)}) collective-permute-start(f32[96,128]{1,0:T(8,128)S(1)} %bitcast_add_fusion.after_ref), channel_id=1, source_target_pairs={{0,32},{16,48},{32,0},{48,16},{64,96},{80,112},{96,64},{112,80},{1... | collective-permute-start | bytes 147464 | tf_op jit(solution)/shard_map/cond/branch_1_fun/ppermute | solution.py:749
  35.0 6.3 %collective-permute-start.4 = (f32[96,128]{1,0:T(8,128)S(1)}, f32[96,128]{1,0:T(8,128)S(1)}, u32[]{:S(2)}, u32[]{:S(2)}) collective-permute-start(f32[96,128]{1,0:T(8,128)S(1)} %add_add_fusion.after_ref), channel_id=1, source_target_pairs={{0,128},{16,144},{32,160},{48,176},{64,192},{80,208},{96,224},{112... | collective-permute-start | bytes 147464 | tf_op jit(solution)/shard_map/cond/branch_1_fun/ppermute | solution.py:749
  36.3 5.4 %collective-permute-start.3 = (f32[96,128]{1,0:T(8,128)S(1)}, f32[96,128]{1,0:T(8,128)S(1)}, u32[]{:S(2)}, u32[]{:S(2)}) collective-permute-start(f32[96,128]{1,0:T(8,128)S(1)} %add_add_fusion.after_ref), channel_id=1, source_target_pairs={{0,192},{16,208},{32,224},{48,240},{64,128},{80,144},{96,160},{112... | collective-permute-start | bytes 147464 | tf_op jit(solution)/shard_map/cond/branch_1_fun/ppermute | solution.py:749
  37.7 4.1 %collective-permute-start.2 = (f32[96,128]{1,0:T(8,128)S(1)}, f32[96,128]{1,0:T(8,128)S(1)}, u32[]{:S(2)}, u32[]{:S(2)}) collective-permute-start(f32[96,128]{1,0:T(8,128)S(1)} %add_add_fusion.after_ref), channel_id=1, source_target_pairs={{0,64},{16,80},{32,96},{48,112},{64,0},{80,16},{96,32},{112,48},{1... | collective-permute-start | bytes 147464 | tf_op jit(solution)/shard_map/cond/branch_1_fun/ppermute | solution.py:749
  43.1 20.4 %all-to-all-start.6 = ((f32[16,16,128]{2,1,0:T(8,128)}), f32[16,16,128]{2,1,0:T(8,128)S(1)}, u32[]{:S(2)}, u32[]{:S(2)}) async-start(f32[16,16,128]{2,1,0:T(8,128)} %get-tuple-element.55), calls=%async_computation.6 | async-start | bytes 262144 | tf_op jit(solution)/shard_map/cond/branch_1_fun/all_to_all | solution.py:788
where the time goes:
time: 97.5 us; the launch traced here: 97.7 us
  Pallas kernels  38.9 us (40%)
  blocking collectives  23.5 us (24%)
  starting transfers between devices  21.3 us (22%)
  waiting for transfers between devices  12 us (12%)
  between operations  1.36 us (1%)
    pallas_call x11, Pallas kernels, run_kernel(): pl.pallas_call(body, out_shape=out_shape, in_specs=scalar_specs + [pl.Blo...  38.9 us
    all_to_all x1, blocking collectives, shared_steps(): shares = lax.all_to_all(mine, 'rep', 0, 0, tiled=True)  14.1 us
    all_to_all x1, starting transfers between devices, shared_steps(): shares = lax.all_to_all(shares, 'rep', 0, 0, tiled=True)  10.9 us
    all_to_all x1, blocking collectives, shared_steps(): lax.all_to_all(partial_forces.reshape(n_blk, 2 * ROWS, BLOCK), 'blk', 0,...  9.4 us
    all_to_all x1, starting transfers between devices, per_device(): gathered = lax.all_to_all(targets, 'blk', 0, 0, tiled=True)  5.56 us
    ppermute x5, starting transfers between devices, from_partner(): return lax.ppermute(value, 'blk', [(i, i ^ distance) for i in range(n_blk)])  4.77 us
    all_to_all x1, waiting for transfers between devices, per_device(): gathered = lax.all_to_all(targets, 'blk', 0, 0, tiled=True)  4.54 us
    all_to_all x1, waiting for transfers between devices, shared_steps(): shares = lax.all_to_all(shares, 'rep', 0, 0, tiled=True)  3.76 us
  transfers between devices with their start and end apart: 7, of which 7 were waited for; matrix products, arithmetic and copies ran while one was open for 1% of the time, Pallas kernels for 12%

commit v1 on v0

--- a/solution.py
+++ b/solution.py
@@ -245,7 +245,7 @@
 
 def active_rows(n_blk, n_rep, list_ref, count_ref):
     per_row = BLOCK // n_rep
-    parts = BLOCK * n_rep // BLOCK // 4
+    parts = n_rep * CAP // per_row
     lanes = lane_iota(n_blk)
     steps = []
     for step in range(STEPS):
@@ -344,7 +344,8 @@
 
 def share_kernel(n_blk, n_rep, list_ref, count_ref, kin_ref, der_ref, last_ref, table_ref, out_ref):
     numbers = share_blocks(n_blk, n_rep, list_ref, count_ref, table_ref)
-    where = [block_at(number) for number in numbers]
+    top = kin_ref.shape[1] // BLOCK - 1
+    where = [block_at(jnp.minimum(number, top)) for number in numbers]
     gap = jnp.zeros((2, BLOCK), F32)
     rows = [
         predicted_block(kin_ref, der_ref, last_ref, where[0], 0.0),

time: 97.5 us -> 96.9 us (level)
  Pallas kernels: 38.9 us -> 37.3 us
    pallas_call x11, Pallas kernels: 38.9 us -> 37.3 us  [run_kernel(): pl.pallas_call(body, out_shape=out_shape, in_specs=scalar_specs + [pl.Blo...]
  transfers between devices with their start and end apart: 7 -> 7, of which waited for: 7 -> 7; matrix products, arithmetic and copies ran while one was open for 1% -> 1% of each run, Pallas kernels for 12% -> 11%
where the time goes in v1:
time: 96.9 us; the launch traced here: 96.4 us
  Pallas kernels  37.3 us (38%)
  blocking collectives  23 us (24%)
  starting transfers between devices  21.3 us (22%)
  waiting for transfers between devices  12.9 us (13%)
  between operations  1.36 us (1%)
    pallas_call x11, Pallas kernels, run_kernel(): pl.pallas_call(body, out_shape=out_shape, in_specs=scalar_specs + [pl.Blo...  37.3 us
    all_to_all x1, blocking collectives, shared_steps(): shares = lax.all_to_all(mine, 'rep', 0, 0, tiled=True)  13.6 us
    all_to_all x1, starting transfers between devices, shared_steps(): shares = lax.all_to_all(shares, 'rep', 0, 0, tiled=True)  10.9 us
    all_to_all x1, blocking collectives, shared_steps(): lax.all_to_all(partial_forces.reshape(n_blk, 2 * ROWS, BLOCK), 'blk', 0,...  9.39 us
    all_to_all x1, starting transfers between devices, per_device(): gathered = lax.all_to_all(targets, 'blk', 0, 0, tiled=True)  5.56 us
    ppermute x5, starting transfers between devices, from_partner(): return lax.ppermute(value, 'blk', [(i, i ^ distance) for i in range(n_blk)])  4.76 us
    all_to_all x1, waiting for transfers between devices, shared_steps(): shares = lax.all_to_all(shares, 'rep', 0, 0, tiled=True)  4.58 us
    all_to_all x1, waiting for transfers between devices, per_device(): gathered = lax.all_to_all(targets, 'blk', 0, 0, tiled=True)  4.54 us
  transfers between devices with their start and end apart: 7, of which 7 were waited for; matrix products, arithmetic and copies ran while one was open for 1% of the time, Pallas kernels for 11%

profile of v1, /device:TPU:32, one launch (start us, length us, event | category | flops | bytes accessed | tf_op | source)
XLA Modules:
  0.0 96.4 jit_solution(8825202060622172767)
XLA Ops:
  0.6 2.4 %shard_map.77 = (s32[8,128]{1,0:T(8,128)S(1)}, f32[16,32,128]{2,1,0:T(8,128)}) custom-call(s32[2,16,2,16]{3,2,1,0:T(2,128)} %bitcast.49, s32[2,16,16]{2,1,0:T(8,128)} %count_ref.1, f32[6,4096]{1,0:T(8,128)} %kin_ref.5, f32[6,4096]{1,0:T(8,128)} %der_ref.5, f32[1,4096]{1,0:T(1,128)} %bitcast.40), custom_call_target="tpu_custom_call" | custom-call | tf_op jit(solution)/shard_map/pallas_call | solution.py:689
  3.0 0.0 copy-start
  3.0 0.0 copy-start.1
  3.0 0.0 copy-start.2
  3.0 0.0 copy-start.3
  3.0 5.6 %all-to-all-start.9 = ((f32[16,32,128]{2,1,0:T(8,128)}), f32[16,32,128]{2,1,0:T(8,128)S(1)}, u32[]{:S(2)}, u32[]{:S(2)}) async-start(f32[16,32,128]{2,1,0:T(8,128)} %get-tuple-element.78), calls=%async_computation.9 | async-start | bytes 524288 | tf_op jit(solution)/shard_map/all_to_all | solution.py:829
  8.6 0.0 copy-done
  8.6 0.0 copy-done.1
  8.6 0.0 copy-done.2
  8.6 0.0 copy-done.3
  8.6 0.9 shard_map.78
  9.5 0.5 slice.3
  10.7 0.0 copy-start.4
  10.7 0.0 copy-start.5
  10.7 1.1 %shard_map.79 = (bf16[4096,128]{1,0:T(8,128)(2,1)S(1)}, bf16[32,4096]{1,0:T(8,128)(2,1)S(1)}) custom-call(s32[8,128]{1,0:T(8,128)S(1)} %get-tuple-element.77.table_ref, f32[6,4096]{1,0:T(8,128)S(1)} %copy-done, f32[6,4096]{1,0:T(8,128)S(1)} %copy-done.1, f32[1,4096]{1,0:T(1,128)S(1)} %bitcast.42, f32[1,4096]{1,0:T(1,128)S(1)} %bitcast.46, ...), custom_call_target="tpu_custom_call" | custom-call | tf_op jit(solution)/shard_map/pallas_call | solution.py:689
  11.7 4.5 %all-to-all-done.9 = f32[16,32,128]{2,1,0:T(8,128)S(1)} async-done(((f32[16,32,128]{2,1,0:T(8,128)}), f32[16,32,128]{2,1,0:T(8,128)S(1)}, u32[]{:S(2)}, u32[]{:S(2)}) %all-to-all-start.9) | async-done | bytes 262176 | tf_op jit(solution)/shard_map/all_to_all | solution.py:829
  16.3 0.0 copy-done.4
  16.3 0.0 copy-done.5
  16.3 80.2 %conditional.1 = ((f32[6,4096]{1,0:T(8,128)}, f32[6,4096]{1,0:T(8,128)})) conditional(s32[]{:T(128)} %bitcast.17, (s32[2,16,16,2]{2,3,1,0:T(2,128)S(1)}, s32[2,16,16]{2,1,0:T(8,128)S(1)}, f32[6,4096]{1,0:T(8,128)S(1)}, f32[6,4096]{1,0:T(8,128)S(1)}, f32[1,4096]{1,0:T(1,128)S(1)}, /*index=5*/f32[1,4096]{1,0:T(1,128)S(1)}) %tuple.30, ...), branch_computations={%region_0.0_spmd, %region_1.0_spmd} | conditional | flops 36864 | bytes 2244848 | solution.py:851
  16.3 13.0 %branch_1_fun.8 = f32[12,8,128]{2,1,0:T(8,128)S(1)} custom-call(s32[8,128]{1,0:T(8,128)S(1)} %get-tuple-element.47.table_ref, f32[64,8,128]{2,1,0:T(8,128)S(1)} %bitcast.36, bf16[4096,128]{1,0:T(8,128)(2,1)S(1)} %get-tuple-element.49.piece_ref, bf16[32,4096]{1,0:T(8,128)(2,1)S(1)} %get-tuple-element.50.moment_ref, f32[6,128]{1,0:T(8,128)S(1)} %get-tuple-element.51.centre_ref), custom_call_target="tpu_custom_call" | custom-call | tf_op jit(solution)/shard_map/cond/branch_1_fun/pallas_call | solution.py:689
  29.3 0.4 collective-permute-start
  29.7 1.1 %collective-permute-done = f32[96,128]{1,0:T(8,128)S(1)} collective-permute-done((f32[96,128]{1,0:T(8,128)S(1)}, f32[96,128]{1,0:T(8,128)S(1)}, u32[]{:S(2)}, u32[]{:S(2)}) %collective-permute-start) | collective-permute-done | bytes 49184 | tf_op jit(solution)/shard_map/cond/branch_1_fun/ppermute | solution.py:750
  30.8 0.8 collective-permute-start.1
  31.6 2.0 %branch_1_fun.9 = (f32[16,8,128]{2,1,0:T(8,128)S(1)}, f32[96,128]{1,0:T(8,128)S(1)}) custom-call(s32[8,128]{1,0:T(8,128)S(1)} %get-tuple-element.47.table_ref, f32[96,128]{1,0:T(8,128)S(1)} %bitcast_add_fusion.after_ref, f32[64,8,128]{2,1,0:T(8,128)S(1)} %bitcast.37, bf16[4096,128]{1,0:T(8,128)(2,1)S(1)} %get-tuple-element.52.piece_ref, ...), custom_call_target="tpu_custom_call" | custom-call | tf_op jit(solution)/shard_map/cond/branch_1_fun/pallas_call | solution.py:689
  33.6 1.4 %collective-permute-done.1 = f32[96,128]{1,0:T(8,128)S(1)} collective-permute-done((f32[96,128]{1,0:T(8,128)S(1)}, f32[96,128]{1,0:T(8,128)S(1)}, u32[]{:S(2)}, u32[]{:S(2)}) %collective-permute-start.1) | collective-permute-done | bytes 49184 | tf_op jit(solution)/shard_map/cond/branch_1_fun/ppermute | solution.py:750
  35.0 1.3 %collective-permute-start.4 = (f32[96,128]{1,0:T(8,128)S(1)}, f32[96,128]{1,0:T(8,128)S(1)}, u32[]{:S(2)}, u32[]{:S(2)}) collective-permute-start(f32[96,128]{1,0:T(8,128)S(1)} %add_add_fusion.after_ref), channel_id=1, source_target_pairs={{0,128},{16,144},{32,160},{48,176},{64,192},{80,208},{96,224},{112... | collective-permute-start | bytes 147464 | tf_op jit(solution)/shard_map/cond/branch_1_fun/ppermute | solution.py:750
  36.3 1.5 %collective-permute-start.3 = (f32[96,128]{1,0:T(8,128)S(1)}, f32[96,128]{1,0:T(8,128)S(1)}, u32[]{:S(2)}, u32[]{:S(2)}) collective-permute-start(f32[96,128]{1,0:T(8,128)S(1)} %add_add_fusion.after_ref), channel_id=1, source_target_pairs={{0,192},{16,208},{32,224},{48,240},{64,128},{80,144},{96,160},{112... | collective-permute-start | bytes 147464 | tf_op jit(solution)/shard_map/cond/branch_1_fun/ppermute | solution.py:750
  37.8 0.8 collective-permute-start.2
  38.6 2.0 %branch_1_fun.10.early_ref.early_b = f32[16,8,128]{2,1,0:T(8,128)S(1)} custom-call(s32[8,128]{1,0:T(8,128)S(1)} %get-tuple-element.47.table_ref, f32[96,128]{1,0:T(8,128)S(1)} %add_add_fusion.after_ref, f32[64,8,128]{2,1,0:T(8,128)S(1)} %bitcast.38, bf16[4096,128]{1,0:T(8,128)(2,1)S(1)} %get-tuple-element.52.piece_ref, ...), custom_call_target="tpu_custom_call" | custom-call | tf_op jit(solution)/shard_map/cond/branch_1_fun/pallas_call | solution.py:689
  40.6 0.7 collective-permute-done.4
  41.2 0.4 collective-permute-done.3
  41.6 0.2 collective-permute-done.2
  41.8 1.3 %branch_1_fun.11 = (f32[16,16,128]{2,1,0:T(8,128)}, f32[12,8,128]{2,1,0:T(8,128)S(1)}) custom-call(s32[8,128]{1,0:T(8,128)S(1)} %get-tuple-element.47.table_ref, f32[12,8,128]{2,1,0:T(8,128)S(1)} %bitcast.30, f32[12,8,128]{2,1,0:T(8,128)S(1)} %bitcast.35, f32[12,8,128]{2,1,0:T(8,128)S(1)} %bitcast.34, f32[12,8,128]{2,1,0:T(8,128)S(1)} %bitcast.33, ...), custom_call_target="tpu_custom_call" | custom-call | tf_op jit(solution)/shard_map/cond/branch_1_fun/pallas_call | solution.py:689
  43.1 10.9 %all-to-all-start.6 = ((f32[16,16,128]{2,1,0:T(8,128)}), f32[16,16,128]{2,1,0:T(8,128)S(1)}, u32[]{:S(2)}, u32[]{:S(2)}) async-start(f32[16,16,128]{2,1,0:T(8,128)} %get-tuple-element.55), calls=%async_computation.6 | async-start | bytes 262144 | tf_op jit(solution)/shard_map/cond/branch_1_fun/all_to_all | solution.py:789
  54.1 4.9 %branch_1_fun.12 = (f32[16,8,128]{2,1,0:T(8,128)S(1)}, f32[16,8,128]{2,1,0:T(8,128)S(1)}) custom-call(s32[8,128]{1,0:T(8,128)S(1)} %get-tuple-element.47.table_ref, f32[12,8,128]{2,1,0:T(8,128)S(1)} %get-tuple-element.56.after_ref, f32[64,8,128]{2,1,0:T(8,128)S(1)} %bitcast.39, bf16[4096,128]{1,0:T(8,128)(2,1)S(1)} %get-tuple-element.52.piece_ref, ...), custom_call_target="tpu_custom_call" | custom-call | tf_op jit(solution)/shard_map/cond/branch_1_fun/pallas_call | solution.py:689
  59.0 4.6 %all-to-all-done.6 = f32[16,16,128]{2,1,0:T(8,128)S(1)} async-done(((f32[16,16,128]{2,1,0:T(8,128)}), f32[16,16,128]{2,1,0:T(8,128)S(1)}, u32[]{:S(2)}, u32[]{:S(2)}) %all-to-all-start.6) | async-done | bytes 131104 | tf_op jit(solution)/shard_map/cond/branch_1_fun/all_to_all | solution.py:789
  63.6 8.3 %branch_1_fun.13 = (f32[32,8,128]{2,1,0:T(8,128)S(1)}, f32[6,4096]{1,0:T(8,128)S(1)}, f32[6,4096]{1,0:T(8,128)S(1)}, f32[1,4096]{1,0:T(1,128)S(1)}) custom-call(s32[8,128]{1,0:T(8,128)S(1)} %get-tuple-element.47.table_ref, f32[32,8,128]{2,1,0:T(8,128)S(1)} %bitcast.29, f32[16,8,128]{2,1,0:T(8,128)S(1)} %get-tuple-element.57.target_ref, ...), custom_call_target="tpu_custom_call" | custom-call | tf_op jit(solution)/shard_map/cond/branch_1_fun/pallas_call | solution.py:689
  71.9 9.4 %all_to_all.46.part_ref = f32[16,16,128]{2,1,0:T(8,128)S(1)} all-to-all(f32[16,16,128]{2,1,0:T(8,128)S(1)} %bitcast.32), channel_id=1, replica_groups=mesh['blk'=16,'rep'=16] {'blk'}, dimensions={0} | all-to-all | bytes 262144 | tf_op jit(solution)/shard_map/cond/branch_1_fun/all_to_all | solution.py:798
  81.3 13.6 %all_to_all.47 = f32[16,16,128]{2,1,0:T(8,128)S(1)} all-to-all(f32[16,16,128]{2,1,0:T(8,128)S(1)} %branch_1_fun.14), channel_id=1, replica_groups=mesh['blk'=16,'rep'=16] {'rep'}, dimensions={0} | all-to-all | bytes 262144 | tf_op jit(solution)/shard_map/cond/branch_1_fun/all_to_all | solution.py:807
  94.9 1.5 %branch_1_fun.15 = (f32[6,4096]{1,0:T(8,128)}, f32[6,4096]{1,0:T(8,128)}) custom-call(s32[8,128]{1,0:T(8,128)S(1)} %get-tuple-element.47.table_ref, f32[32,8,128]{2,1,0:T(8,128)S(1)} %bitcast.24, f32[6,4096]{1,0:T(8,128)S(1)} %get-tuple-element.65.kin_ref, f32[6,4096]{1,0:T(8,128)S(1)} %get-tuple-element.66.der_ref, f32[1,4096]{1,0:T(1,128)S(1)} %get-tuple-element.67.last_ref), custom_call_target="tpu_custom_call" | custom-call | tf_op jit(solution)/shard_map/cond/branch_1_fun/pallas_call | solution.py:689
  (3 shorter events, 0.0 us)
Async XLA Ops:
  3.0 5.6 %copy-start = (f32[6,4096]{1,0:T(8,128)S(1)}, f32[6,4096]{1,0:T(8,128)}, u32[]{:S(2)}) copy-start(f32[6,4096]{1,0:T(8,128)} %kin_ref.5) | copy-start | bytes 294916
  3.0 5.6 %copy-start.1 = (f32[6,4096]{1,0:T(8,128)S(1)}, f32[6,4096]{1,0:T(8,128)}, u32[]{:S(2)}) copy-start(f32[6,4096]{1,0:T(8,128)} %der_ref.5) | copy-start | bytes 294916
  3.0 5.6 %copy-start.2 = (f32[4096]{0:T(1024)S(1)}, f32[4096]{0:T(1024)}, u32[]{:S(2)}) copy-start(f32[4096]{0:T(1024)} %param.11) | copy-start | bytes 49156
  3.0 5.6 %copy-start.3 = (f32[4096]{0:T(1024)S(1)}, f32[4096]{0:T(1024)}, u32[]{:S(2)}) copy-start(f32[4096]{0:T(1024)} %param.10) | copy-start | bytes 49156
  3.0 13.3 %all-to-all-start.9 = ((f32[16,32,128]{2,1,0:T(8,128)}), f32[16,32,128]{2,1,0:T(8,128)S(1)}, u32[]{:S(2)}, u32[]{:S(2)}) async-start(f32[16,32,128]{2,1,0:T(8,128)} %get-tuple-element.78), calls=%async_computation.9 | async-start | bytes 524288 | tf_op jit(solution)/shard_map/all_to_all | solution.py:829
  10.7 5.6 %copy-start.4 = (s32[2,16,16,2]{2,3,1,0:T(2,128)S(1)}, s32[2,16,16,2]{2,3,1,0:T(2,128)}, u32[]{:S(2)}) copy-start(s32[2,16,16,2]{2,3,1,0:T(2,128)} %param.12) | copy-start | bytes 12292
  10.7 5.6 %copy-start.5 = (s32[2,16,16]{2,1,0:T(8,128)S(1)}, s32[2,16,16]{2,1,0:T(8,128)}, u32[]{:S(2)}) copy-start(s32[2,16,16]{2,1,0:T(8,128)} %count_ref.1) | copy-start | bytes 6148
  29.3 1.5 %collective-permute-start = (f32[96,128]{1,0:T(8,128)S(1)}, f32[96,128]{1,0:T(8,128)S(1)}, u32[]{:S(2)}, u32[]{:S(2)}) collective-permute-start(f32[96,128]{1,0:T(8,128)S(1)} %bitcast.31), channel_id=1, source_target_pairs={{0,16},{16,0},{32,48},{48,32},{64,80},{80,64},{96,112},{112,96},{1... | collective-permute-start | bytes 147464 | tf_op jit(solution)/shard_map/cond/branch_1_fun/ppermute | solution.py:750
  30.8 4.2 %collective-permute-start.1 = (f32[96,128]{1,0:T(8,128)S(1)}, f32[96,128]{1,0:T(8,128)S(1)}, u32[]{:S(2)}, u32[]{:S(2)}) collective-permute-start(f32[96,128]{1,0:T(8,128)S(1)} %bitcast_add_fusion.after_ref), channel_id=1, source_target_pairs={{0,32},{16,48},{32,0},{48,16},{64,96},{80,112},{96,64},{112,80},{1... | collective-permute-start | bytes 147464 | tf_op jit(solution)/shard_map/cond/branch_1_fun/ppermute | solution.py:750
  35.0 6.3 %collective-permute-start.4 = (f32[96,128]{1,0:T(8,128)S(1)}, f32[96,128]{1,0:T(8,128)S(1)}, u32[]{:S(2)}, u32[]{:S(2)}) collective-permute-start(f32[96,128]{1,0:T(8,128)S(1)} %add_add_fusion.after_ref), channel_id=1, source_target_pairs={{0,128},{16,144},{32,160},{48,176},{64,192},{80,208},{96,224},{112... | collective-permute-start | bytes 147464 | tf_op jit(solution)/shard_map/cond/branch_1_fun/ppermute | solution.py:750
  36.3 5.4 %collective-permute-start.3 = (f32[96,128]{1,0:T(8,128)S(1)}, f32[96,128]{1,0:T(8,128)S(1)}, u32[]{:S(2)}, u32[]{:S(2)}) collective-permute-start(f32[96,128]{1,0:T(8,128)S(1)} %add_add_fusion.after_ref), channel_id=1, source_target_pairs={{0,192},{16,208},{32,224},{48,240},{64,128},{80,144},{96,160},{112... | collective-permute-start | bytes 147464 | tf_op jit(solution)/shard_map/cond/branch_1_fun/ppermute | solution.py:750
  37.8 4.1 %collective-permute-start.2 = (f32[96,128]{1,0:T(8,128)S(1)}, f32[96,128]{1,0:T(8,128)S(1)}, u32[]{:S(2)}, u32[]{:S(2)}) collective-permute-start(f32[96,128]{1,0:T(8,128)S(1)} %add_add_fusion.after_ref), channel_id=1, source_target_pairs={{0,64},{16,80},{32,96},{48,112},{64,0},{80,16},{96,32},{112,48},{1... | collective-permute-start | bytes 147464 | tf_op jit(solution)/shard_map/cond/branch_1_fun/ppermute | solution.py:750
  43.1 20.4 %all-to-all-start.6 = ((f32[16,16,128]{2,1,0:T(8,128)}), f32[16,16,128]{2,1,0:T(8,128)S(1)}, u32[]{:S(2)}, u32[]{:S(2)}) async-start(f32[16,16,128]{2,1,0:T(8,128)} %get-tuple-element.55), calls=%async_computation.6 | async-start | bytes 262144 | tf_op jit(solution)/shard_map/cond/branch_1_fun/all_to_all | solution.py:789
